TPU v7x, 32 devices: a whole 2x2x4 slice. The times are simulated.
32 devices in a mesh: groups: 2 (over y), ctx: 16 (over z, x, core), dp: 1.
Axes of the slice: x: 2, y: 2, z: 4, core: 2. Of those that a mesh axis runs over, the one named last changes fastest.
Arguments:
- tokens: bfloat16 [4096, 1024], P(('groups', 'ctx', 'dp')), parts along dimension 0, may hold values from -6 to 6
- cotangent: bfloat16 [4096, 1024], P(('groups', 'ctx', 'dp')), parts along dimension 0, may hold values from -6 to 6
- expert_ids: int32 [4096, 8], P(('groups', 'ctx', 'dp')), parts along dimension 0, may hold values from 0 to 15, all different within a row; in each aligned block of 128 rows (0 to 127, 128 to 255, ...) at most 80 rows name the same one
- router_weights: float32 [4096, 8], P(('groups', 'ctx', 'dp')), parts along dimension 0, may hold values from 0.03 to 0.3
- seq_lengths: int32 [8], P('groups'), parts along dimension 0, may hold values from 256 to 768, as said below
- w_gate: bfloat16 [16, 1024, 384], P('ctx', 'dp'), may hold values from -0.1875 to 0.1875
- w_up: bfloat16 [16, 1024, 384], P('ctx', 'dp'), may hold values from -0.1875 to 0.1875
- w_down: bfloat16 [16, 384, 1024], P('ctx', None, 'dp'), may hold values from -0.3125 to 0.3125
Outputs:
- mixed: bfloat16 [4096, 1024], P(('groups', 'ctx', 'dp')), parts along dimension 0
- token_grads: bfloat16 [4096, 1024], P(('groups', 'ctx', 'dp')), parts along dimension 0
- weight_grads: float32 [4096, 8], P(('groups', 'ctx', 'dp')), parts along dimension 0
There are 2 independent parts, one for each index of `groups`. A program takes and returns all parts, laid end to end along the dimension named above; an argument that names none is the same for every part. Nothing has to cross between parts.
Inputs may be any that keep to these rules, and one draw needn't show every extreme that they name: `expert_ids`: in each aligned block of 128 rows (the rows of one device) every expert is named by at most 80 rows, and in every draw some expert is named by exactly 80 rows of some block; the 8 entries of a row differ. `seq_lengths`: the 4 lengths sum to 2048; both ends of the range are reached in every draw.
All inputs are finite; a program needn't handle non-finite values.
Results may differ from a plain program's by a relative error of at most 0.0064.
Values may be sent and summed in bfloat16 or wider, within the bound.
A program may use at most 128 MiB of HBM per device.

v0:
```python
import jax
import jax.numpy as jnp
from jax import lax
from jax.sharding import PartitionSpec as P


def loss_scale(position, seq_lengths, mean_length):
    ends = jnp.cumsum(seq_lengths)
    starts = ends - seq_lengths
    inside = (position[:, None] >= starts[None, :]) & (position[:, None] < ends[None, :])
    own_length = jnp.sum(jnp.where(inside, seq_lengths[None, :], 0), axis=1)
    return mean_length / own_length.astype(jnp.float32)


def forward_rows(slot_rows, gate_full, up_full, down_full):
    gate_pre = jnp.dot(slot_rows, gate_full, preferred_element_type=jnp.float32)
    up_value = jnp.dot(slot_rows, up_full, preferred_element_type=jnp.float32)
    activated = jax.nn.silu(gate_pre)
    hidden = (activated * up_value).astype(jnp.bfloat16)
    expert_out = jnp.dot(hidden, down_full, preferred_element_type=jnp.float32).astype(jnp.bfloat16)
    return (gate_pre, up_value, activated, expert_out)


def backward_rows(grad_rows, gate_pre, up_value, activated, gate_full, up_full, down_full):
    contract = (((1,), (1,)), ((), ()))
    hidden_grad = lax.dot_general(
        grad_rows, down_full, contract, preferred_element_type=jnp.float32
    )
    sigmoid_value = jax.nn.sigmoid(gate_pre)
    silu_slope = sigmoid_value * (1.0 + gate_pre * (1.0 - sigmoid_value))
    gate_grad = (hidden_grad * up_value * silu_slope).astype(jnp.bfloat16)
    up_grad = (hidden_grad * activated).astype(jnp.bfloat16)
    slot_grad = lax.dot_general(gate_grad, gate_full, contract, preferred_element_type=jnp.float32)
    slot_grad = slot_grad + lax.dot_general(
        up_grad, up_full, contract, preferred_element_type=jnp.float32
    )
    return slot_grad.astype(jnp.bfloat16)


def slot_ranks(flat_ids, experts):
    expert_hits = (flat_ids[:, None] == jnp.arange(experts, dtype=jnp.int32)[None, :]).astype(
        jnp.int32
    )
    assign_count = flat_ids.shape[0]
    row_iota = lax.broadcasted_iota(jnp.int32, (assign_count, assign_count), 0)
    col_iota = lax.broadcasted_iota(jnp.int32, (assign_count, assign_count), 1)
    lower_mask = (row_iota > col_iota).astype(jnp.bfloat16)
    earlier = jnp.dot(
        lower_mask, expert_hits.astype(jnp.bfloat16), preferred_element_type=jnp.float32
    )
    return jnp.sum(earlier * expert_hits.astype(jnp.float32), axis=1).astype(jnp.int32)


def per_device(tokens, cotangent, expert_ids, router_weights, seq_lengths, w_gate, w_up, w_down):
    ctx_count = lax.axis_size("ctx")
    dp_count = lax.axis_size("dp")
    row_count, top_count = expert_ids.shape
    slot_cap = max(2, min(row_count, row_count * top_count * 5 // (4 * ctx_count)))
    block_index = lax.axis_index("ctx") * dp_count + lax.axis_index("dp")
    position = block_index * row_count + jnp.arange(row_count, dtype=jnp.int32)
    loss_weight = loss_scale(position, seq_lengths, row_count * 4.0)
    out_grad = (cotangent.astype(jnp.float32) * loss_weight[:, None]).astype(jnp.bfloat16)
    flat_ids = expert_ids.reshape(-1)
    assign_count = flat_ids.shape[0]
    dest_slot = flat_ids * slot_cap + slot_ranks(flat_ids, ctx_count)
    source_row = jnp.full((ctx_count * slot_cap,), assign_count, jnp.int32)
    source_row = source_row.at[dest_slot].set(jnp.arange(assign_count, dtype=jnp.int32))
    filled = source_row < assign_count
    token_of = jnp.minimum(source_row, assign_count - 1) // top_count
    zero_value = jnp.zeros((), jnp.bfloat16)
    token_send = jnp.where(filled[:, None], tokens[token_of], zero_value).reshape(
        ctx_count, slot_cap, -1
    )
    grad_send = jnp.where(filled[:, None], out_grad[token_of], zero_value).reshape(
        ctx_count, slot_cap, -1
    )
    gate_full, up_full, down_full = (
        lax.all_gather(w_gate[0], "dp", axis=0, tiled=True),
        lax.all_gather(w_up[0], "dp", axis=0, tiled=True),
        lax.all_gather(w_down[0], "dp", axis=1, tiled=True),
    )
    token_arrived = lax.all_to_all(token_send, "ctx", split_axis=0, concat_axis=0, tiled=True)
    grad_arrived = lax.all_to_all(grad_send, "ctx", split_axis=0, concat_axis=0, tiled=True)
    source_count = token_arrived.shape[0]
    slot_count = token_arrived.shape[1]
    slot_rows = token_arrived.reshape(source_count * slot_count, -1)
    grad_rows = grad_arrived.reshape(source_count * slot_count, -1)
    gate_pre, up_value, activated, expert_out = forward_rows(
        slot_rows, gate_full, up_full, down_full
    )
    out_blocks = expert_out.reshape(source_count, slot_count, -1)
    slot_grad = backward_rows(
        grad_rows, gate_pre, up_value, activated, gate_full, up_full, down_full
    )
    out_home = lax.all_to_all(out_blocks, "ctx", split_axis=0, concat_axis=0, tiled=True)
    grad_home = lax.all_to_all(
        slot_grad.reshape(source_count, slot_count, -1),
        "ctx",
        split_axis=0,
        concat_axis=0,
        tiled=True,
    )
    out_rows = out_home.reshape(ctx_count * slot_cap, -1)[dest_slot].reshape(
        row_count, top_count, -1
    )
    grad_rows = grad_home.reshape(ctx_count * slot_cap, -1)[dest_slot].reshape(
        row_count, top_count, -1
    )
    mixed = jnp.sum(router_weights[:, :, None] * out_rows.astype(jnp.float32), axis=1).astype(
        jnp.bfloat16
    )
    token_grads = jnp.sum(
        router_weights[:, :, None] * grad_rows.astype(jnp.float32), axis=1
    ).astype(jnp.bfloat16)
    weight_grads = jnp.einsum("td,tkd->tk", out_grad, out_rows, preferred_element_type=jnp.float32)
    return (mixed, token_grads, weight_grads)


def solution(mesh):
    in_specs = (
        P(("groups", "ctx", "dp"), None),
        P(("groups", "ctx", "dp"), None),
        P(("groups", "ctx", "dp"), None),
        P(("groups", "ctx", "dp"), None),
        P("groups"),
        P("ctx", "dp", None),
        P("ctx", "dp", None),
        P("ctx", None, "dp"),
    )
    out_specs = (
        P(("groups", "ctx", "dp"), None),
        P(("groups", "ctx", "dp"), None),
        P(("groups", "ctx", "dp"), None),
    )
    return jax.shard_map(
        per_device, mesh=mesh, in_specs=in_specs, out_specs=out_specs, check_vma=False
    )
```

profile of v0, /device:TPU:11, one launch (start us, length us, event | category | flops | bytes accessed | tf_op | source)
XLA Modules:
  0.0 306.6 jit_solution(6240023815004228532)
XLA Ops:
  0.6 0.9 copy.17
  3.0 4.3 %scatter_custom_fusion = s32[1280]{0:T(1024)S(1)} fusion(s32[1024]{0:T(1024)S(1)} %bitcast.49, s32[1024]{0:T(1024)S(1)} %iota.24, s32[]{:T(128)} %constant.15.clone.1), kind=kCustom, calls=%fused_computation.51 | custom fusion | bytes 5124 | tf_op jit(solution)/shard_map/scatter | solution.py:67
  9.6 1.1 multiply_convert_fusion.6
  10.7 5.1 %gather_fusion.2 = bf16[1280,1024]{1,0:T(8,128)(2,1)} fusion(bf16[128,1024]{1,0:T(8,128)(2,1)S(1)} %multiply_convert_fusion.6, s32[2048]{0:T(1024)S(1)} %pad_clamp_fusion), kind=kCustom, calls=%fused_computation.2 | custom fusion | bytes 5248000 | tf_op jit(solution)/shard_map/gather | solution.py:74
  15.8 5.1 %gather_fusion = bf16[1280,1024]{1,0:T(8,128)(2,1)} fusion(bf16[128,1024]{1,0:T(8,128)(2,1)S(1)} %copy-done.1, s32[2048]{0:T(1024)S(1)} %pad_clamp_fusion), kind=kCustom, calls=%fused_computation | custom fusion | bytes 5248000 | tf_op jit(solution)/shard_map/gather | solution.py:71
  21.0 3.8 %broadcast_select_fusion = (bf16[16,80,1024]{2,1,0:T(8,128)(2,1)}, bf16[16,80,1024]{2,1,0:T(8,128)(2,1)S(1)}) fusion(bf16[16,80,1024]{2,1,0:T(8,128)(2,1)} %bitcast.42, pred[16,80]{1,0:T(8,128)(4,1)S(1)} %broadcast_in_dim.48, bf16[16,80,1024]{2,1,0:T(8,128)(2,1)} %bitcast.43), kind=kLoop, calls=%fused_computation.12 | loop fusion | flops 2621440 | bytes 10487040 | tf_op jit(solution)/shard_map/jit(_where)/select_n | solution.py:74
  24.8 65.0 %all_to_all.20 = bf16[16,80,1024]{2,1,0:T(8,128)(2,1)} all-to-all(bf16[16,80,1024]{2,1,0:T(8,128)(2,1)S(1)} %get-tuple-element.6), channel_id=1, replica_groups=mesh['groups'=2,'ctx'=16,'dp'=1] {'ctx'}, dimensions={0} | all-to-all | bytes 5242880 | tf_op jit(solution)/shard_map/all_to_all | solution.py:82
  89.8 5.2 %all-to-all-start.2 = ((bf16[16,80,1024]{2,1,0:T(8,128)(2,1)}), bf16[16,80,1024]{2,1,0:T(8,128)(2,1)S(1)}, u32[]{:S(2)}, u32[]{:S(2)}) async-start(bf16[16,80,1024]{2,1,0:T(8,128)(2,1)} %get-tuple-element.5), calls=%async_computation.2 | async-start | bytes 5242880 | tf_op jit(solution)/shard_map/all_to_all | solution.py:83
  95.0 4.7 %fusion.16 = f32[1280,384]{1,0:T(8,128)} fusion(bf16[1280,1024]{1,0:T(8,128)(2,1)} %bitcast.47, bf16[1,1024,384]{2,1,0:T(8,128)(2,1)S(1)} %copy-done), kind=kOutput, calls=%fused_computation.32 | convolution fusion | flops 1006632960 | bytes 5373952 | tf_op jit(solution)/shard_map/dot_general | solution.py:16
  99.7 2.9 fusion.13
  102.6 51.0 %all-to-all-done.2 = bf16[16,80,1024]{2,1,0:T(8,128)(2,1)S(1)} async-done(((bf16[16,80,1024]{2,1,0:T(8,128)(2,1)}), bf16[16,80,1024]{2,1,0:T(8,128)(2,1)S(1)}, u32[]{:S(2)}, u32[]{:S(2)}) %all-to-all-start.2) | async-done | bytes 2621472 | tf_op jit(solution)/shard_map/all_to_all | solution.py:83
  153.6 2.8 fusion.9
  156.5 1.8 fusion.7
  158.3 3.1 %add_convert_fusion = bf16[1280,1024]{1,0:T(8,128)(2,1)} fusion(f32[1280,1024]{1,0:T(8,128)S(1)} %fusion.7, f32[1280,384]{1,0:T(8,128)S(1)} %fusion.9, bf16[1,1024,384]{2,1,0:T(8,128)(2,1)S(1)} %copy-done.7, f32[1280,384]{1,0:T(8,128)S(1)} %copy-done.8), kind=kOutput, calls=%fused_computation.5 | convolution fusion | flops 1012203520 | bytes 12582912 | tf_op jit(solution)/shard_map/dot_general | solution.py:34
  161.5 4.9 %all-to-all-start.3 = ((bf16[16,80,1024]{2,1,0:T(8,128)(2,1)}), bf16[16,80,1024]{2,1,0:T(8,128)(2,1)S(1)}, u32[]{:S(2)}, u32[]{:S(2)}) async-start(bf16[16,80,1024]{2,1,0:T(8,128)(2,1)} %bitcast.46), calls=%async_computation.3 | async-start | bytes 5242880 | tf_op jit(solution)/shard_map/all_to_all | solution.py:96
  166.4 5.4 %convolution_convert_fusion = bf16[1280,1024]{1,0:T(8,128)(2,1)} fusion(f32[1280,384]{1,0:T(8,128)} %fusion.13, bf16[1,384,1024]{2,1,0:T(8,128)(2,1)} %param.15, f32[1280,384]{1,0:T(8,128)} %fusion.16), kind=kOutput, calls=%fused_computation.11 | convolution fusion | flops 1010892800 | bytes 7340032 | tf_op jit(solution)/shard_map/dot_general | solution.py:20
  171.8 53.3 %all-to-all-done.3 = bf16[16,80,1024]{2,1,0:T(8,128)(2,1)S(1)} async-done(((bf16[16,80,1024]{2,1,0:T(8,128)(2,1)}), bf16[16,80,1024]{2,1,0:T(8,128)(2,1)S(1)}, u32[]{:S(2)}, u32[]{:S(2)}) %all-to-all-start.3) | async-done | bytes 2621472 | tf_op jit(solution)/shard_map/all_to_all | solution.py:96
  225.0 5.0 %all-to-all-start.1 = ((bf16[16,80,1024]{2,1,0:T(8,128)(2,1)}), bf16[16,80,1024]{2,1,0:T(8,128)(2,1)}, u32[]{:S(2)}, u32[]{:S(2)}) async-start(bf16[16,80,1024]{2,1,0:T(8,128)(2,1)} %bitcast.44), calls=%async_computation.1 | async-start | bytes 5242880 | tf_op jit(solution)/shard_map/all_to_all | solution.py:95
  230.2 1.8 fusion.32
  231.9 5.4 %gather_fusion.3 = bf16[1024,1024]{1,0:T(8,128)(2,1)} fusion(bf16[1280,1024]{1,0:T(8,128)(2,1)S(1)} %bitcast.41, s32[1024]{0:T(1024)S(1)} %broadcast_clamp_fusion), kind=kCustom, calls=%fused_computation.3 | custom fusion | bytes 4198400 | tf_op jit(solution)/shard_map/gather | solution.py:106
  237.3 51.5 %all-to-all-done.1 = bf16[16,80,1024]{2,1,0:T(8,128)(2,1)} async-done(((bf16[16,80,1024]{2,1,0:T(8,128)(2,1)}), bf16[16,80,1024]{2,1,0:T(8,128)(2,1)}, u32[]{:S(2)}, u32[]{:S(2)}) %all-to-all-start.1) | async-done | bytes 2621472 | tf_op jit(solution)/shard_map/all_to_all | solution.py:95
  288.8 8.1 %gather_fusion.1 = bf16[1024,1024]{1,0:T(8,128)(2,1)} fusion(bf16[1280,1024]{1,0:T(8,128)(2,1)} %bitcast.8, s32[1024]{0:T(1024)S(1)} %broadcast_clamp_fusion), kind=kCustom, calls=%fused_computation.1 | custom fusion | bytes 4198400 | tf_op jit(solution)/shard_map/gather | solution.py:103
  297.0 3.0 fusion.2
  300.6 6.0 %fusion = (bf16[128,1024]{1,0:T(8,128)(2,1)}, bf16[128,1024]{1,0:T(8,128)(2,1)}) fusion(bf16[1024,1024]{1,0:T(8,128)(2,1)S(1)} %copy-done.2, f32[128,8]{1,0:T(8,128)S(1)} %copy.15, bf16[1024,1024]{1,0:T(8,128)(2,1)} %gather_fusion.1), kind=kLoop, calls=%fused_computation.7 | loop fusion | flops 6029312 | bytes 4722688 | tf_op jit(solution)/shard_map/reduce_sum | solution.py:112
  (40 shorter events, 4.7 us)
Async XLA Ops:
  0.6 94.3 %copy-start = (bf16[1,1024,384]{2,1,0:T(8,128)(2,1)S(1)}, bf16[1,1024,384]{2,1,0:T(8,128)(2,1)}, u32[]{:S(2)}) copy-start(bf16[1,1024,384]{2,1,0:T(8,128)(2,1)} %param.13) | copy-start | bytes 2359300
  10.7 5.1 %copy-start.1 = (bf16[128,1024]{1,0:T(8,128)(2,1)S(1)}, bf16[128,1024]{1,0:T(8,128)(2,1)}, u32[]{:S(2)}) copy-start(bf16[128,1024]{1,0:T(8,128)(2,1)} %param.8) | copy-start | bytes 786436
  89.8 63.8 %all-to-all-start.2 = ((bf16[16,80,1024]{2,1,0:T(8,128)(2,1)}), bf16[16,80,1024]{2,1,0:T(8,128)(2,1)S(1)}, u32[]{:S(2)}, u32[]{:S(2)}) async-start(bf16[16,80,1024]{2,1,0:T(8,128)(2,1)} %get-tuple-element.5), calls=%async_computation.2 | async-start | bytes 5242880 | tf_op jit(solution)/shard_map/all_to_all | solution.py:83
  95.0 4.8 %copy-start.3 = (bf16[16,80,1024]{2,1,0:T(8,128)(2,1)S(1)}, bf16[16,80,1024]{2,1,0:T(8,128)(2,1)}, u32[]{:S(2)}) copy-start(bf16[16,80,1024]{2,1,0:T(8,128)(2,1)} %all_to_all.20) | copy-start | bytes 7864324
  95.0 4.7 %copy-start.6 = (bf16[1,1024,384]{2,1,0:T(8,128)(2,1)S(1)}, bf16[1,1024,384]{2,1,0:T(8,128)(2,1)}, u32[]{:S(2)}) copy-start(bf16[1,1024,384]{2,1,0:T(8,128)(2,1)} %param.14) | copy-start | bytes 2359300
  153.6 2.9 copy-start.8
  153.6 2.9 copy-start.9
  156.5 1.8 copy-start.7
  161.5 63.6 %all-to-all-start.3 = ((bf16[16,80,1024]{2,1,0:T(8,128)(2,1)}), bf16[16,80,1024]{2,1,0:T(8,128)(2,1)S(1)}, u32[]{:S(2)}, u32[]{:S(2)}) async-start(bf16[16,80,1024]{2,1,0:T(8,128)(2,1)} %bitcast.46), calls=%async_computation.3 | async-start | bytes 5242880 | tf_op jit(solution)/shard_map/all_to_all | solution.py:96
  225.0 5.0 %copy-start.5 = (f32[128,8]{0,1:T(8,128)S(1)}, f32[128,8]{0,1:T(8,128)}, u32[]{:S(2)}) copy-start(f32[128,8]{0,1:T(8,128)} %param.11) | copy-start | bytes 12292
  225.0 63.8 %all-to-all-start.1 = ((bf16[16,80,1024]{2,1,0:T(8,128)(2,1)}), bf16[16,80,1024]{2,1,0:T(8,128)(2,1)}, u32[]{:S(2)}, u32[]{:S(2)}) async-start(bf16[16,80,1024]{2,1,0:T(8,128)(2,1)} %bitcast.44), calls=%async_computation.1 | async-start | bytes 5242880 | tf_op jit(solution)/shard_map/all_to_all | solution.py:95
  288.8 8.1 %copy-start.4 = (bf16[128,1024,1]{1,0,2:T(8,128)(2,1)S(1)}, bf16[128,1024,1]{1,0,2:T(8,128)(2,1)}, u32[]{:S(2)}) copy-start(bf16[128,1024,1]{1,0,2:T(8,128)(2,1)} %fusion.32) | copy-start | bytes 786436
  297.0 3.6 %copy-start.2 = (bf16[1024,1024]{1,0:T(8,128)(2,1)S(1)}, bf16[1024,1024]{1,0:T(8,128)(2,1)}, u32[]{:S(2)}) copy-start(bf16[1024,1024]{1,0:T(8,128)(2,1)} %gather_fusion.3) | copy-start | bytes 6291460
where the time goes:
time: 307 us
  waiting for transfers between devices  156 us (51%)
  blocking collectives  65 us (21%)
  local copies, waits for them, and re-layouts  30 us (10%)
  matrix products  24.2 us (8%)
  other arithmetic  15.7 us (5%)
  starting transfers between devices  15.1 us (5%)
    all_to_all x1, blocking collectives, per_device(): lax.all_to_all(token_send, 'ctx', split_axis=0, concat_axis=0, tiled=True)  65 us
    all_to_all x1, waiting for transfers between devices, per_device(): lax.all_to_all(slot_grad.reshape(source_count, slot_count, -1), 'ctx', sp...  53.3 us
    all_to_all x1, waiting for transfers between devices, per_device(): lax.all_to_all(out_blocks, 'ctx', split_axis=0, concat_axis=0, tiled=True)  51.5 us
    all_to_all x1, waiting for transfers between devices, per_device(): lax.all_to_all(grad_send, 'ctx', split_axis=0, concat_axis=0, tiled=True)  51 us
    gather x1, local copies, waits for them, and re-layouts, per_device(): out_home.reshape(ctx_count * slot_cap, -1)[dest_slot]  8.13 us
  transfers between devices with their start and end apart: 3, of which 3 were waited for; matrix products, arithmetic and copies ran while one was open for 7% of the time, Pallas kernels for 0%

commit v1 on v0

--- a/solution.py
+++ b/solution.py
@@ -1,7 +1,359 @@
+import functools
+
 import jax
 import jax.numpy as jnp
 from jax import lax
+from jax.experimental import pallas as pl
+from jax.experimental.pallas import tpu as pltpu
 from jax.sharding import PartitionSpec as P
+
+MESH = pl.DeviceIdType.MESH
+NT = (((1,), (1,)), ((), ()))
+F32 = jnp.float32
+BF16 = jnp.bfloat16
+
+
+def ring_kernel(
+    n,
+    mean_length,
+    seq_ref,
+    tok_ref,
+    cot_ref,
+    ids_ref,
+    rw_ref,
+    gate_ref,
+    up_ref,
+    down_ref,
+    mixed_ref,
+    tgrad_ref,
+    wgrad_ref,
+    rows_in,
+    out,
+    pair_in,
+    ring_in,
+    w_send,
+    w_in,
+    w_col,
+    g_send,
+    g_in,
+    ag_send,
+    ag_recv,
+    pair_send,
+    pair_recv,
+    op_send,
+    op_recv,
+    rs_send,
+    rs_recv,
+    w_sems,
+    g_sems,
+):
+    rows, depth = tok_ref.shape
+    top = ids_ref.shape[1]
+    chips = n // 2
+    half = chips // 2
+    me = lax.axis_index("ctx")
+    core = me % 2
+    chip = me // 2
+    side = chip % 2
+    pos = (chip // 2) * (1 - side) + (chips - 1 - chip // 2) * side
+
+    def device(back, plane):
+        at = (pos + chips - back) % chips
+        far = at // half
+        other = 2 * (at * (1 - far) + (chips - 1 - at) * far) + far
+        cc = core if plane == 0 else 1 - core
+        return {"ctx": 2 * other + cc}
+
+    def device_index(back, plane):
+        return device(back, plane)["ctx"]
+
+    right, left, partner = device(chips - 1, 0), device(1, 0), device(0, 1)
+    peers = [(o, p) for o in range(chips) for p in range(2) if (o, p) != (0, 0)]
+
+    barrier = pltpu.get_barrier_semaphore()
+    for o, p in peers:
+        pl.semaphore_signal(barrier, inc=1, device_id=device(o, p), device_id_type=MESH)
+
+    rows_in[0, 0, 0:rows, :] = tok_ref[...]
+    place = me * rows + lax.broadcasted_iota(jnp.int32, (rows, 128), 0)
+    own_length = jnp.zeros((rows, 128), jnp.int32)
+    begin = jnp.int32(0)
+    for i in range(seq_ref.shape[0]):
+        size = seq_ref[i]
+        own_length = jnp.where((place >= begin) & (place < begin + size), size, own_length)
+        begin = begin + size
+    loss_weight = (mean_length / own_length.astype(F32))[:, 0:1]
+    rows_in[1, 0, 0:rows, :] = (cot_ref[...].astype(F32) * loss_weight).astype(BF16)
+    ids = ids_ref[...]
+    weights = rw_ref[...]
+    expert_lane = lax.broadcasted_iota(jnp.int32, (rows, 8 * n), 1) // 8
+    by_expert = jnp.zeros((rows, 8 * n), F32)
+    for k in range(top):
+        by_expert = by_expert + jnp.where(ids[:, k : k + 1] == expert_lane, weights[:, k : k + 1], 0.0)
+    w_send[...] = by_expert.T.reshape(n, 8, rows)
+
+    pl.semaphore_wait(barrier, len(peers))
+
+    def w_copy(o, p):
+        return pltpu.make_async_remote_copy(
+            src_ref=w_send.at[device_index(o, p)],
+            dst_ref=w_in.at[2 * ((chips - o) % chips) + p],
+            send_sem=w_sems.at[0],
+            recv_sem=w_sems.at[1],
+            device_id=device(o, p),
+            device_id_type=MESH,
+        )
+
+    def ag_copy(a, src, dst, to):
+        return pltpu.make_async_remote_copy(
+            src_ref=rows_in.at[a, src, 0:rows],
+            dst_ref=rows_in.at[a, dst, 0:rows],
+            send_sem=ag_send.at[a, dst],
+            recv_sem=ag_recv.at[a, dst],
+            device_id=to,
+            device_id_type=MESH,
+        )
+
+    def pair_copy(a, o):
+        return pltpu.make_async_remote_copy(
+            src_ref=rows_in.at[a, o, 0:rows],
+            dst_ref=rows_in.at[a, o, rows : 2 * rows],
+            send_sem=pair_send.at[a, o],
+            recv_sem=pair_recv.at[a, o],
+            device_id=partner,
+            device_id_type=MESH,
+        )
+
+    def op_copy(a, o):
+        return pltpu.make_async_remote_copy(
+            src_ref=out.at[a, o, rows : 2 * rows],
+            dst_ref=pair_in.at[a, o],
+            send_sem=op_send.at[a, o],
+            recv_sem=op_recv.at[a, o],
+            device_id=partner,
+            device_id_type=MESH,
+        )
+
+    def rs_copy(a, o, leftward):
+        return pltpu.make_async_remote_copy(
+            src_ref=out.at[a, o, 0:rows],
+            dst_ref=ring_in.at[a, o - 1 if leftward else o + 1],
+            send_sem=rs_send.at[a, o],
+            recv_sem=rs_recv.at[a, o - 1 if leftward else o + 1],
+            device_id=left if leftward else right,
+            device_id_type=MESH,
+        )
+
+    def g_copy(o, p):
+        return pltpu.make_async_remote_copy(
+            src_ref=g_send.at[2 * o + p],
+            dst_ref=g_in.at[me],
+            send_sem=g_sems.at[0],
+            recv_sem=g_sems.at[1],
+            device_id=device(o, p),
+            device_id_type=MESH,
+        )
+
+    for a in range(2):
+        ag_copy(a, 0, 1, right).start()
+        ag_copy(a, 0, chips - 1, left).start()
+    for a in range(2):
+        pair_copy(a, 0).start()
+    for o, p in peers:
+        w_copy(o, p).start()
+    w_in[0] = w_send[me]
+
+    def column(o, p):
+        lane = lax.broadcasted_iota(jnp.int32, (rows, 8 * n), 1)
+        return jnp.sum(jnp.where(lane == (2 * o + p) * 8, w_col[...], 0.0), axis=1, keepdims=True)
+
+    def compute(o):
+        x = rows_in[0, o]
+        g = rows_in[1, o]
+        weight = jnp.concatenate([column(o, 0), column(o, 1)], axis=0)
+        gate_pre = jnp.dot(x, gate_ref[0], preferred_element_type=F32)
+        up_value = jnp.dot(x, up_ref[0], preferred_element_type=F32)
+        hidden_grad = lax.dot_general(g, down_ref[0], NT, preferred_element_type=F32)
+        sig = 0.5 * jnp.tanh(0.5 * gate_pre) + 0.5
+        act = gate_pre * sig
+        hidden = act * up_value
+        inner = (hidden * hidden_grad).astype(BF16)
+        ones = jnp.ones((8, inner.shape[1]), BF16)
+        inner_rows = lax.dot_general(ones, inner, NT, preferred_element_type=F32)
+        g_send[2 * o] = inner_rows[:, 0:rows]
+        g_send[2 * o + 1] = inner_rows[:, rows : 2 * rows]
+        out[0, o] = jnp.dot(
+            (hidden * weight).astype(BF16), down_ref[0], preferred_element_type=F32
+        ).astype(BF16)
+        scaled = hidden_grad * weight
+        gate_grad = (scaled * up_value * (sig * (1.0 + gate_pre * (1.0 - sig)))).astype(BF16)
+        up_grad = (scaled * act).astype(BF16)
+        slot_grad = lax.dot_general(gate_grad, gate_ref[0], NT, preferred_element_type=F32)
+        slot_grad = slot_grad + lax.dot_general(up_grad, up_ref[0], NT, preferred_element_type=F32)
+        out[1, o] = slot_grad.astype(BF16)
+
+    for a in range(2):
+        pair_copy(a, 0).wait_recv()
+    every_w = pltpu.make_async_copy(w_in.at[1:n], w_in.at[1:n], w_sems.at[1])
+    every_w.wait()
+    w_col[...] = w_in[...].reshape(8 * n, rows).T
+
+    compute(0)
+    for a in range(2):
+        op_copy(a, 0).start()
+
+    @pl.loop(1, half)
+    def _(s):
+        back = chips - s
+        for a in range(2):
+            ag_copy(a, s - 1, s, right).wait_recv()
+            if a == 0:
+                ag_copy(a, s, s + 1, right).start()
+            else:
+                @pl.when(s < half - 1)
+                def _():
+                    ag_copy(a, s, s + 1, right).start()
+            pair_copy(a, s).start()
+            ag_copy(a, s, back, left).wait_recv()
+            if a == 1:
+                ag_copy(a, back, back - 1, left).start()
+            else:
+                @pl.when(s < half - 1)
+                def _():
+                    ag_copy(a, back, back - 1, left).start()
+            pair_copy(a, back).start()
+        for a in range(2):
+            pair_copy(a, s).wait_recv()
+            pair_copy(a, back).wait_recv()
+
+        @pl.loop(0, 2)
+        def _(j):
+            o = s * (1 - j) + back * j
+            compute(o)
+            for a in range(2):
+                op_copy(a, o).start()
+
+    def step(a, o, leftward, arrived):
+        op_copy(a, o).wait_recv()
+        total = out[a, o, 0:rows].astype(F32) + pair_in[a, o].astype(F32)
+        if arrived:
+            rs_copy(a, o + 1 if leftward else o - 1, leftward).wait_recv()
+            total = total + ring_in[a, o].astype(F32)
+        out[a, o, 0:rows] = total.astype(BF16)
+        rs_copy(a, o, leftward).start()
+
+    ag_copy(0, half - 1, half, right).wait_recv()
+    pair_copy(0, half).start()
+    ag_copy(1, half + 1, half, left).wait_recv()
+    pair_copy(1, half).start()
+    step(0, half + 1, False, False)
+    step(1, half - 1, True, False)
+    for a in range(2):
+        pair_copy(a, half).wait_recv()
+    compute(half)
+    op_copy(1, half).start()
+    op_copy(0, half).start()
+    for o, p in peers:
+        g_copy(o, p).start()
+    g_in[me] = g_send[0]
+    step(1, half, False, False)
+    step(0, half, True, False)
+    for d in range(1, half):
+        if d + 1 < half:
+            step(0, half + d + 1, False, True)
+            step(1, half - d - 1, True, True)
+        step(1, half + d, False, True)
+        step(0, half - d, True, True)
+
+    every_g = pltpu.make_async_copy(g_in.at[1:n], g_in.at[1:n], g_sems.at[1])
+    every_g.wait()
+    by_token = g_in[...].reshape(8 * n, rows).T
+    lane = lax.broadcasted_iota(jnp.int32, (rows, 8 * n), 1)
+    top_lane = lax.broadcasted_iota(jnp.int32, (rows, top), 1)
+    picked = jnp.zeros((rows, top), F32)
+    for k in range(top):
+        value = jnp.sum(jnp.where(lane == ids[:, k : k + 1] * 8, by_token, 0.0), axis=1, keepdims=True)
+        picked = jnp.where(top_lane == k, value, picked)
+    wgrad_ref[...] = picked
+
+    for a, result in ((0, mixed_ref), (1, tgrad_ref)):
+        op_copy(a, 0).wait_recv()
+        total = out[a, 0, 0:rows].astype(F32) + pair_in[a, 0].astype(F32)
+        rs_copy(a, chips - 1, False).wait_recv()
+        total = total + ring_in[a, chips].astype(F32)
+        rs_copy(a, 1, True).wait_recv()
+        total = total + ring_in[a, 0].astype(F32)
+        result[...] = total.astype(BF16)
+
+    for a in range(2):
+        for s in range(1, chips):
+            ag_copy(a, 0, s, right).wait_send()
+            rs_copy(a, s, s < half).wait_send()
+        for o in range(chips):
+            pair_copy(a, o).wait_send()
+            op_copy(a, o).wait_send()
+    pltpu.make_async_copy(w_send.at[1:n], w_send.at[1:n], w_sems.at[0]).wait()
+    pltpu.make_async_copy(g_send.at[1:n], g_send.at[1:n], g_sems.at[0]).wait()
+
+
+def ring_device(tokens, cotangent, expert_ids, router_weights, seq_lengths, w_gate, w_up, w_down):
+    n = lax.axis_size("ctx")
+    chips = n // 2
+    rows, depth = tokens.shape
+    vmem = pl.BlockSpec(memory_space=pltpu.VMEM)
+    dma = pltpu.SemaphoreType.DMA
+    return pl.pallas_call(
+        functools.partial(ring_kernel, n, rows * 4.0),
+        out_shape=(
+            jax.ShapeDtypeStruct(tokens.shape, BF16),
+            jax.ShapeDtypeStruct(tokens.shape, BF16),
+            jax.ShapeDtypeStruct(router_weights.shape, F32),
+        ),
+        in_specs=[pl.BlockSpec(memory_space=pltpu.SMEM)] + [vmem] * 7,
+        out_specs=(vmem, vmem, vmem),
+        scratch_shapes=[
+            pltpu.VMEM((2, chips, 2 * rows, depth), BF16),
+            pltpu.VMEM((2, chips, 2 * rows, depth), BF16),
+            pltpu.VMEM((2, chips, rows, depth), BF16),
+            pltpu.VMEM((2, chips + 1, rows, depth), BF16),
+            pltpu.VMEM((n, 8, rows), F32),
+            pltpu.VMEM((n, 8, rows), F32),
+            pltpu.VMEM((rows, 8 * n), F32),
+            pltpu.VMEM((n, 8, rows), F32),
+            pltpu.VMEM((n, 8, rows), F32),
+            dma((2, chips)),
+            dma((2, chips)),
+            dma((2, chips)),
+            dma((2, chips)),
+            dma((2, chips)),
+            dma((2, chips)),
+            dma((2, chips)),
+            dma((2, chips + 1)),
+            dma((2,)),
+            dma((2,)),
+        ],
+        compiler_params=pltpu.CompilerParams(
+            collective_id=0, has_side_effects=True, vmem_limit_bytes=52 * 1024 * 1024
+        ),
+        cost_estimate=pl.CostEstimate(
+            flops=12 * n * rows * w_gate.size, bytes_accessed=6 * w_gate.size, transcendentals=0
+        ),
+    )(seq_lengths, tokens, cotangent, expert_ids, router_weights, w_gate, w_up, w_down)
+
+
+def ring_fits(mesh, arrays):
+    tokens, _, expert_ids, _, _, w_gate = arrays[:6]
+    n = mesh.shape["ctx"]
+    rows = tokens.shape[0] // (mesh.shape["groups"] * n * mesh.shape["dp"])
+    held = 2 * n * rows * tokens.shape[1] * 2 * 4
+    return (
+        mesh.shape["dp"] == 1
+        and w_gate.shape[0] == n
+        and n % 4 == 0
+        and n >= 8
+        and rows % 128 == 0
+        and held <= 40 * 1024 * 1024
+    )
 
 
 def loss_scale(position, seq_lengths, mean_length):
@@ -132,6 +484,11 @@
         P(("groups", "ctx", "dp"), None),
         P(("groups", "ctx", "dp"), None),
     )
-    return jax.shard_map(
-        per_device, mesh=mesh, in_specs=in_specs, out_specs=out_specs, check_vma=False
-    )
+
+    def run(*arrays):
+        plan = ring_device if ring_fits(mesh, arrays) else per_device
+        return jax.shard_map(
+            plan, mesh=mesh, in_specs=in_specs, out_specs=out_specs, check_vma=False
+        )(*arrays)
+
+    return run

time: 307 us -> 107 us (0.35)
  the two profiles are of different devices: /device:TPU:11 before, /device:TPU:0 now
where the time goes in v1:
time: 107 us
  Pallas kernels  101 us (94%)
  local copies, waits for them, and re-layouts  5.41 us (5%)
    pallas_call x1, Pallas kernels, ring_device(): pl.pallas_call(functools.partial(ring_kernel, n, rows * 4.0), out_shape=(...  101 us
    unnamed x12, local copies, waits for them, and re-layouts  4.75 us

profile of v1, /device:TPU:0, one launch (start us, length us, event | category | flops | bytes accessed | tf_op | source)
XLA Modules:
  0.0 107.0 jit_solution(9831019196228985128)
XLA Ops:
  0.6 0.0 copy-start.3
  0.6 0.8 copy.11.ids_ref
  1.4 0.0 copy-done.3
  1.4 0.0 copy-start.2
  1.4 0.1 copy.12.rw_ref
  1.6 0.5 copy-done.2
  2.1 0.0 copy-start
  2.1 0.9 copy-done
  3.0 0.0 copy-start.1
  3.0 0.9 copy-done.1
  4.0 100.9 %shard_map.103 = (bf16[128,1024]{1,0:T(8,128)(2,1)S(1)}, bf16[128,1024]{1,0:T(8,128)(2,1)S(1)}, f32[128,8]{1,0:T(8,128)S(1)}) custom-call(s32[4]{0:T(128)S(1)} %copy-done.2, bf16[128,1024]{1,0:T(8,128)(2,1)S(1)} %copy-done, bf16[128,1024]{1,0:T(8,128)(2,1)S(1)} %copy-done.1, s32[128,8]{1,0:T(8,128)S(1)} %copy.11.ids_ref, f32[128,8]{1,0:T(8,128)S(1)} %copy.12.rw_ref, ...), custom_call_target="tpu_custom_call" | custom-call | flops 9663676416 | bytes 2359296 | tf_op jit(solution)/shard_map/pallas_call | solution.py:305
  104.9 0.7 copy.13
  105.5 0.7 copy.16
  106.3 0.7 copy.17
Async XLA Ops:
  0.6 0.8 copy-start.3
  1.4 0.7 copy-start.2
  2.1 0.9 copy-start
  3.0 0.9 copy-start.1

commit v2 on v0

--- a/solution.py
+++ b/solution.py
@@ -1,7 +1,508 @@
+import functools
+
 import jax
 import jax.numpy as jnp
 from jax import lax
+from jax.experimental import pallas as pl
+from jax.experimental.pallas import tpu as pltpu
 from jax.sharding import PartitionSpec as P
+
+MESH = pl.DeviceIdType.MESH
+NT = (((1,), (1,)), ((), ()))
+F32 = jnp.float32
+BF16 = jnp.bfloat16
+
+
+def line_kernel(
+    n,
+    mean_length,
+    seq_ref,
+    tok_ref,
+    cot_ref,
+    ids_ref,
+    rw_ref,
+    gate_hbm,
+    up_hbm,
+    down_hbm,
+    mixed_ref,
+    tgrad_ref,
+    wgrad_ref,
+    gate_ref,
+    up_ref,
+    down_ref,
+    rows_in,
+    acc,
+    out,
+    pair_in,
+    line_in,
+    w_send,
+    w_in,
+    w_col,
+    g_send,
+    g_in,
+    load_sems,
+    x_send,
+    x_recv,
+    y_send,
+    y_recv,
+    ag_send,
+    ag_recv,
+    pair_send,
+    pair_recv,
+    op_send,
+    op_recv,
+    rs_send,
+    rs_recv,
+    w_sems,
+    g_sems,
+):
+    rows, depth = tok_ref.shape
+    top = ids_ref.shape[0]
+    planes = n // 4
+    me = lax.axis_index("ctx")
+    group = lax.axis_index("groups")
+    core = me % 2
+    side = (me // 2) % 2
+    z = me // 4
+
+    def at(zz, plane):
+        cc = core if plane == 0 else 1 - core
+        return {"groups": group, "ctx": (zz * 2 + side) * 2 + cc}
+
+    partner = at(z, 1)
+    x_mate = {"groups": group, "ctx": (z * 2 + 1 - side) * 2 + core}
+    y_mate = {"groups": 1 - group, "ctx": me}
+    above, below = at((z + 1) % planes, 0), at((z + planes - 1) % planes, 0)
+    line = [(d, p) for d in range(planes) for p in range(2) if (d, p) != (0, 0)]
+
+    barrier = pltpu.get_barrier_semaphore()
+    for to in [at((z + d) % planes, p) for d, p in line] + [x_mate, y_mate]:
+        pl.semaphore_signal(barrier, inc=1, device_id=to, device_id_type=MESH)
+
+    parts = ((gate_hbm, gate_ref), (up_hbm, up_ref), (down_hbm, down_ref))
+    loads = [
+        pltpu.make_async_copy(src.at[0], dst.at[0], load_sems.at[i])
+        for i, (src, dst) in enumerate(parts)
+    ]
+    for load in loads:
+        load.start()
+
+    rows_in[0, z, 0:rows, :] = tok_ref[...]
+    place = me * rows + lax.broadcasted_iota(jnp.int32, (rows, 128), 0)
+    own_length = jnp.zeros((rows, 128), jnp.int32)
+    begin = jnp.int32(0)
+    for i in range(seq_ref.shape[0]):
+        size = seq_ref[i]
+        own_length = jnp.where((place >= begin) & (place < begin + size), size, own_length)
+        begin = begin + size
+    loss_weight = (mean_length / own_length.astype(F32))[:, 0:1]
+    rows_in[1, z, 0:rows, :] = (cot_ref[...].astype(F32) * loss_weight).astype(BF16)
+
+    pl.semaphore_wait(barrier, len(line) + 2)
+
+    def ag_copy(a, slot, to):
+        return pltpu.make_async_remote_copy(
+            src_ref=rows_in.at[a, slot, 0:rows],
+            dst_ref=rows_in.at[a, slot, 0:rows],
+            send_sem=ag_send.at[a, slot, 0 if to is above else 1],
+            recv_sem=ag_recv.at[a, slot],
+            device_id=to,
+            device_id_type=MESH,
+        )
+
+    def pair_copy(a, slot):
+        return pltpu.make_async_remote_copy(
+            src_ref=rows_in.at[a, slot, 0:rows],
+            dst_ref=rows_in.at[a, slot, rows : 2 * rows],
+            send_sem=pair_send.at[a, slot],
+            recv_sem=pair_recv.at[a, slot],
+            device_id=partner,
+            device_id_type=MESH,
+        )
+
+    def op_copy(a, slot):
+        return pltpu.make_async_remote_copy(
+            src_ref=out.at[a, slot, rows : 2 * rows],
+            dst_ref=pair_in.at[a, slot],
+            send_sem=op_send.at[a, slot],
+            recv_sem=op_recv.at[a, slot],
+            device_id=partner,
+            device_id_type=MESH,
+        )
+
+    def rs_copy(a, slot, arrive, to):
+        return pltpu.make_async_remote_copy(
+            src_ref=out.at[a, slot, 0:rows],
+            dst_ref=line_in.at[a, arrive],
+            send_sem=rs_send.at[a, slot],
+            recv_sem=rs_recv.at[a, arrive],
+            device_id=to,
+            device_id_type=MESH,
+        )
+
+    def half_of(i, which):
+        count = parts[i][1].shape[1] // 2
+        return pl.ds(pl.multiple_of(which * count, count), count)
+
+    def x_copy(i):
+        return pltpu.make_async_remote_copy(
+            src_ref=parts[i][0].at[0, half_of(i, group)],
+            dst_ref=parts[i][1].at[1, half_of(i, group)],
+            send_sem=x_send.at[i],
+            recv_sem=x_recv.at[i],
+            device_id=x_mate,
+            device_id_type=MESH,
+        )
+
+    def y_copy(i):
+        return pltpu.make_async_remote_copy(
+            src_ref=parts[i][1].at[1, half_of(i, group)],
+            dst_ref=parts[i][1].at[1, half_of(i, group)],
+            send_sem=y_send.at[i],
+            recv_sem=y_recv.at[i],
+            device_id=y_mate,
+            device_id_type=MESH,
+        )
+
+    def w_copy(d, p):
+        there = (z + d) % planes
+        return pltpu.make_async_remote_copy(
+            src_ref=w_send.at[2 * there + (core if p == 0 else 1 - core)],
+            dst_ref=w_in.at[2 * z + p],
+            send_sem=w_sems.at[0],
+            recv_sem=w_sems.at[1],
+            device_id=at(there, p),
+            device_id_type=MESH,
+        )
+
+    def g_copy(d, p):
+        there = (z + d) % planes
+        return pltpu.make_async_remote_copy(
+            src_ref=g_send.at[2 * there + p],
+            dst_ref=g_in.at[2 * z + core],
+            send_sem=g_sems.at[0],
+            recv_sem=g_sems.at[1],
+            device_id=at(there, p),
+            device_id_type=MESH,
+        )
+
+    def send_on(a, slot, upward):
+        if upward:
+            @pl.when(z < planes - 1)
+            def _():
+                ag_copy(a, slot, above).start()
+        else:
+            @pl.when(z > 0)
+            def _():
+                ag_copy(a, slot, below).start()
+
+    for a in range(2):
+        send_on(a, z, True)
+        send_on(a, z, False)
+    for i in range(3):
+        x_copy(i).start()
+    for a in range(2):
+        pair_copy(a, z).start()
+
+    shape = (8 * n, rows)
+    place_of = lax.broadcasted_iota(jnp.int32, shape, 0) // 8
+    expert_of = (place_of // 4 * 2 + place_of % 2) * 2 + place_of // 2 % 2
+    by_expert = jnp.zeros(shape, F32)
+    for k in range(top):
+        by_expert = by_expert + jnp.where(ids_ref[k : k + 1, :] == expert_of, rw_ref[k : k + 1, :], 0.0)
+    w_send[...] = by_expert.reshape(n // 2, 2, 8, rows)
+    for d, p in line:
+        w_copy(d, p).start()
+    w_in[2 * z] = w_send[2 * z + core]
+
+    for load in loads:
+        load.wait()
+    for a in range(2):
+        pair_copy(a, z).wait_recv()
+    every = w_in.at[1 : 2 * planes]
+    pltpu.make_async_copy(every, every, w_sems.at[1]).wait()
+    w_col[...] = w_in[...].reshape(8 * n, rows).T
+
+    def column(slot, p, whose):
+        lane = lax.broadcasted_iota(jnp.int32, (rows, 8 * n), 1)
+        wanted = ((2 * slot + p) * 2 + whose) * 8
+        return jnp.sum(jnp.where(lane == wanted, w_col[...], 0.0), axis=1, keepdims=True)
+
+    def compute(e, slot):
+        whose = side if e == 0 else 1 - side
+        x = rows_in[0, slot]
+        g = rows_in[1, slot]
+        weight = jnp.concatenate([column(slot, 0, whose), column(slot, 1, whose)], axis=0)
+        gate_pre = jnp.dot(x, gate_ref[e], preferred_element_type=F32)
+        up_value = jnp.dot(x, up_ref[e], preferred_element_type=F32)
+        hidden_grad = lax.dot_general(g, down_ref[e], NT, preferred_element_type=F32)
+        sig = 0.5 * jnp.tanh(0.5 * gate_pre) + 0.5
+        act = gate_pre * sig
+        hidden = act * up_value
+        inner = (hidden * hidden_grad).astype(BF16)
+        ones = jnp.ones((8, inner.shape[1]), BF16)
+        inner_rows = lax.dot_general(ones, inner, NT, preferred_element_type=F32)
+        g_send[2 * slot, whose] = inner_rows[:, 0:rows]
+        g_send[2 * slot + 1, whose] = inner_rows[:, rows : 2 * rows]
+        mix = jnp.dot((hidden * weight).astype(BF16), down_ref[e], preferred_element_type=F32)
+        scaled = hidden_grad * weight
+        gate_grad = (scaled * up_value * (sig * (1.0 + gate_pre * (1.0 - sig)))).astype(BF16)
+        up_grad = (scaled * act).astype(BF16)
+        slot_grad = lax.dot_general(gate_grad, gate_ref[e], NT, preferred_element_type=F32)
+        slot_grad = slot_grad + lax.dot_general(up_grad, up_ref[e], NT, preferred_element_type=F32)
+        if e == 0:
+            acc[0, slot] = mix
+            acc[1, slot] = slot_grad
+        else:
+            out[0, slot] = (acc[0, slot] + mix).astype(BF16)
+            out[1, slot] = (acc[1, slot] + slot_grad).astype(BF16)
+            for a in range(2):
+                op_copy(a, slot).start()
+
+    def arrivals(s):
+        for a in range(2):
+            @pl.when(z - s >= 0)
+            def _():
+                ag_copy(a, z - s, above).wait_recv()
+                send_on(a, z - s, True)
+                pair_copy(a, z - s).start()
+
+            @pl.when(z + s < planes)
+            def _():
+                ag_copy(a, z + s, below).wait_recv()
+                send_on(a, z + s, False)
+                pair_copy(a, z + s).start()
+
+    def first_pass(s):
+        @pl.loop(0, 2)
+        def _(j):
+            slot = z - s + 2 * s * j
+
+            @pl.when((slot >= 0) & (slot < planes))
+            def _():
+                for a in range(2):
+                    pair_copy(a, slot).wait_recv()
+                compute(0, slot)
+
+    def pass_on(i):
+        x_copy(i).wait_recv()
+        y_copy(i).start()
+
+    def line_step(dest, upward, wanted):
+        first = 0 if upward else planes - 1
+
+        def send(a):
+            if upward:
+                @pl.when(z + 1 == dest)
+                def _():
+                    rs_copy(a, dest, planes, above).start()
+
+                @pl.when(z + 1 != dest)
+                def _():
+                    rs_copy(a, dest, dest, above).start()
+            else:
+                rs_copy(a, dest, dest, below).start()
+
+        def add(a, arrived):
+            op_copy(a, dest).wait_recv()
+            total = out[a, dest, 0:rows].astype(F32) + pair_in[a, dest].astype(F32)
+            if arrived:
+                rs_copy(a, dest, dest, above).wait_recv()
+                total = total + line_in[a, dest].astype(F32)
+            out[a, dest, 0:rows] = total.astype(BF16)
+            send(a)
+
+        @pl.when(wanted & (z < dest if upward else z > dest))
+        def _():
+            @pl.when(z != first)
+            def _():
+                for a in range(2):
+                    add(a, True)
+
+            @pl.when(z == first)
+            def _():
+                for a in range(2):
+                    add(a, False)
+
+    upward = [planes - 2, planes - 1] + list(range(planes - 3, 0, -1))
+    table = []
+    for zz in range(planes):
+        low = zz < planes // 2
+        order = [u if low else planes - 1 - u for u in upward + [0]]
+        table.append([u for u in order if u != zz] + [zz])
+
+    def turn(k):
+        slot = 0
+        for zz in range(planes):
+            slot = slot + table[zz][k] * (z == zz).astype(jnp.int32)
+        return slot
+
+    compute(0, z)
+    last = planes - 1
+    for s in range(1, last):
+        arrivals(s)
+        if s <= 2:
+            pass_on(s - 1)
+        first_pass(s)
+    pass_on(2)
+    for i in range(3):
+        y_copy(i).wait_recv()
+    compute(1, turn(0))
+    arrivals(last)
+    inner = (z > 0) & (z < last)
+    high = z >= planes // 2
+    for k, u in enumerate(upward):
+        line_step(planes - 1 - u, False, high)
+        line_step(u, True, z >= 0)
+        line_step(planes - 1 - u, False, z < planes // 2)
+        if k == 0:
+            first_pass(last)
+
+            @pl.loop(1, 4)
+            def _(j):
+                slot = 0
+                for jj in range(1, 4):
+                    slot = slot + turn(jj) * (j == jj).astype(jnp.int32)
+
+                @pl.when((j < 3) | inner)
+                def _():
+                    compute(1, slot)
+        elif k == 1:
+            @pl.when((z == 0) | (z == last))
+            def _():
+                compute(1, turn(3))
+        elif k + 2 < planes:
+            compute(1, turn(k + 2))
+    for d, p in line:
+        g_copy(d, p).start()
+    g_in[2 * z + core] = g_send[2 * z]
+
+    every = g_in.at[1 : 2 * planes]
+    pltpu.make_async_copy(every, every, g_sems.at[1]).wait()
+    ids = ids_ref[...]
+    picked = jnp.zeros((top, rows), F32)
+    for e in range(n):
+        picked = jnp.where(ids == e, g_in[e // 4 * 2 + e % 2, e // 2 % 2][0:top], picked)
+    wgrad_ref[...] = picked
+
+    for a in range(2):
+        op_copy(a, z).wait_recv()
+        total = out[a, z, 0:rows].astype(F32) + pair_in[a, z].astype(F32)
+        acc[a, z, 0:rows] = total
+
+        @pl.when(z > 0)
+        def _():
+            rs_copy(a, z, planes, above).wait_recv()
+            acc[a, z, 0:rows] = acc[a, z, 0:rows] + line_in[a, planes].astype(F32)
+
+        @pl.when(z < planes - 1)
+        def _():
+            rs_copy(a, z, z, below).wait_recv()
+            acc[a, z, 0:rows] = acc[a, z, 0:rows] + line_in[a, z].astype(F32)
+
+    mixed_ref[...] = acc[0, z, 0:rows].astype(BF16)
+    tgrad_ref[...] = acc[1, z, 0:rows].astype(BF16)
+
+    for a in range(2):
+        for slot in range(planes):
+            @pl.when((slot <= z) & (z < planes - 1))
+            def _():
+                ag_copy(a, slot, above).wait_send()
+
+            @pl.when((slot >= z) & (z > 0))
+            def _():
+                ag_copy(a, slot, below).wait_send()
+
+            @pl.when(slot != z)
+            def _():
+                rs_copy(a, slot, slot, above).wait_send()
+
+            pair_copy(a, slot).wait_send()
+            op_copy(a, slot).wait_send()
+    for i in range(3):
+        x_copy(i).wait_send()
+        y_copy(i).wait_send()
+    every = w_send.at[1 : 2 * planes]
+    pltpu.make_async_copy(every, every, w_sems.at[0]).wait()
+    every = g_send.at[1 : 2 * planes]
+    pltpu.make_async_copy(every, every, g_sems.at[0]).wait()
+
+
+def line_device(tokens, cotangent, expert_ids, router_weights, seq_lengths, w_gate, w_up, w_down):
+    n = lax.axis_size("ctx")
+    planes = n // 4
+    rows, depth = tokens.shape
+    hidden = w_gate.shape[2]
+    top = expert_ids.shape[1]
+    vmem = pl.BlockSpec(memory_space=pltpu.VMEM)
+    hbm = pl.BlockSpec(memory_space=pl.ANY)
+    dma = pltpu.SemaphoreType.DMA
+    mixed, token_grads, weight_grads = pl.pallas_call(
+        functools.partial(line_kernel, n, rows * 4.0),
+        out_shape=(
+            jax.ShapeDtypeStruct(tokens.shape, BF16),
+            jax.ShapeDtypeStruct(tokens.shape, BF16),
+            jax.ShapeDtypeStruct((top, rows), F32),
+        ),
+        in_specs=[pl.BlockSpec(memory_space=pltpu.SMEM)] + [vmem] * 4 + [hbm] * 3,
+        out_specs=(vmem, vmem, vmem),
+        scratch_shapes=[
+            pltpu.VMEM((2, depth, hidden), BF16),
+            pltpu.VMEM((2, depth, hidden), BF16),
+            pltpu.VMEM((2, hidden, depth), BF16),
+            pltpu.VMEM((2, planes, 2 * rows, depth), BF16),
+            pltpu.VMEM((2, planes, 2 * rows, depth), F32),
+            pltpu.VMEM((2, planes, 2 * rows, depth), BF16),
+            pltpu.VMEM((2, planes, rows, depth), BF16),
+            pltpu.VMEM((2, planes + 1, rows, depth), BF16),
+            pltpu.VMEM((n // 2, 2, 8, rows), F32),
+            pltpu.VMEM((n // 2, 2, 8, rows), F32),
+            pltpu.VMEM((rows, 8 * n), F32),
+            pltpu.VMEM((n // 2, 2, 8, rows), F32),
+            pltpu.VMEM((n // 2, 2, 8, rows), F32),
+            dma((3,)),
+            dma((3,)),
+            dma((3,)),
+            dma((3,)),
+            dma((3,)),
+            dma((2, planes, 2)),
+            dma((2, planes)),
+            dma((2, planes)),
+            dma((2, planes)),
+            dma((2, planes)),
+            dma((2, planes)),
+            dma((2, planes)),
+            dma((2, planes + 1)),
+            dma((2,)),
+            dma((2,)),
+        ],
+        compiler_params=pltpu.CompilerParams(
+            collective_id=0, has_side_effects=True, vmem_limit_bytes=52 * 1024 * 1024
+        ),
+        cost_estimate=pl.CostEstimate(
+            flops=12 * n * rows * w_gate.size, bytes_accessed=6 * w_gate.size, transcendentals=0
+        ),
+    )(seq_lengths, tokens, cotangent, expert_ids.T, router_weights.T, w_gate, w_up, w_down)
+    return mixed, token_grads, weight_grads.T
+
+
+def line_fits(mesh, arrays):
+    tokens, _, expert_ids, _, _, w_gate = arrays[:6]
+    n = mesh.shape["ctx"]
+    rows = tokens.shape[0] // (mesh.shape["groups"] * n * mesh.shape["dp"])
+    held = 2 * n * rows * tokens.shape[1] * 9
+    return (
+        mesh.shape["dp"] == 1
+        and mesh.shape["groups"] == 2
+        and w_gate.shape[0] == n
+        and w_gate.shape[1] % 32 == 0
+        and w_gate.shape[2] % 32 == 0
+        and n % 8 == 0
+        and n >= 16
+        and expert_ids.shape[1] <= 8
+        and rows % 128 == 0
+        and held <= 40 * 1024 * 1024
+    )
 
 
 def loss_scale(position, seq_lengths, mean_length):
@@ -132,6 +633,11 @@
         P(("groups", "ctx", "dp"), None),
         P(("groups", "ctx", "dp"), None),
     )
-    return jax.shard_map(
-        per_device, mesh=mesh, in_specs=in_specs, out_specs=out_specs, check_vma=False
-    )
+
+    def run(*arrays):
+        plan = line_device if line_fits(mesh, arrays) else per_device
+        return jax.shard_map(
+            plan, mesh=mesh, in_specs=in_specs, out_specs=out_specs, check_vma=False
+        )(*arrays)
+
+    return run

time: 307 us -> 107 us (0.35)
  the two profiles are of different devices: /device:TPU:11 before, /device:TPU:0 now
where the time goes in v2:
time: 107 us
  Pallas kernels  99.3 us (93%)
  local copies, waits for them, and re-layouts  7.05 us (7%)
    pallas_call x1, Pallas kernels, line_device(): pl.pallas_call(functools.partial(line_kernel, n, rows * 4.0), out_shape=(...  99.3 us
    unnamed x15, local copies, waits for them, and re-layouts  7.05 us

profile of v2, /device:TPU:0, one launch (start us, length us, event | category | flops | bytes accessed | tf_op | source)
XLA Modules:
  0.0 107.0 jit_solution(5257548912582200437)
XLA Ops:
  0.6 0.0 copy-start.5
  0.6 0.6 copy-done.5
  1.3 0.0 copy-start
  1.3 1.1 %copy-done = bf16[1,1024,384]{2,1,0:T(8,128)(2,1)S(1)} copy-done((bf16[1,1024,384]{2,1,0:T(8,128)(2,1)S(1)}, bf16[1,1024,384]{2,1,0:T(8,128)(2,1)}, u32[]{:S(2)}) %copy-start) | copy-done | bytes 786456
  2.4 0.0 copy-start.1
  2.4 0.9 copy-done.1
  3.4 0.0 copy-start.2
  3.4 0.9 copy-done.2
  4.3 0.0 copy-start.3
  4.3 0.7 copy-done.3
  5.0 0.0 copy-start.4
  5.0 0.7 copy-done.4
  5.7 99.3 %shard_map.103 = (bf16[128,1024]{1,0:T(8,128)(2,1)S(1)}, bf16[128,1024]{1,0:T(8,128)(2,1)S(1)}, f32[8,128]{1,0:T(8,128)S(1)}) custom-call(s32[4]{0:T(128)S(1)} %copy-done.5, bf16[128,1024]{1,0:T(8,128)(2,1)S(1)} %copy-done.1, bf16[128,1024]{1,0:T(8,128)(2,1)S(1)} %copy-done.2, s32[8,128]{1,0:T(8,128)S(1)} %bitcast.4, f32[8,128]{1,0:T(8,128)S(1)} %bitcast.5, ...), custom_call_target="tpu_custom_call" | custom-call | flops 9663676416 | bytes 2359296 | tf_op jit(solution)/shard_map/pallas_call | solution.py:440
  105.0 0.7 copy.14
  105.7 0.7 copy.15
  106.4 0.6 copy.16
Async XLA Ops:
  0.6 0.7 copy-start.5
  1.3 1.1 %copy-start = (bf16[1,1024,384]{2,1,0:T(8,128)(2,1)S(1)}, bf16[1,1024,384]{2,1,0:T(8,128)(2,1)}, u32[]{:S(2)}) copy-start(bf16[1,1024,384]{2,1,0:T(8,128)(2,1)} %gate_hbm.1) | copy-start | bytes 2359300
  2.4 0.9 copy-start.1
  3.4 0.9 copy-start.2
  4.3 0.7 copy-start.3
  5.0 0.7 copy-start.4

commit v3 on v2

--- a/solution.py
+++ b/solution.py
@@ -17,8 +17,8 @@
     n,
     mean_length,
     seq_ref,
-    tok_ref,
-    cot_ref,
+    tok_hbm,
+    cot_hbm,
     ids_ref,
     rw_ref,
     gate_hbm,
@@ -27,9 +27,9 @@
     mixed_ref,
     tgrad_ref,
     wgrad_ref,
-    gate_ref,
-    up_ref,
+    both_ref,
     down_ref,
+    cot_ref,
     rows_in,
     acc,
     out,
@@ -56,7 +56,8 @@
     w_sems,
     g_sems,
 ):
-    rows, depth = tok_ref.shape
+    rows, depth = tok_hbm.shape
+    wide = gate_hbm.shape[2]
     top = ids_ref.shape[0]
     planes = n // 4
     me = lax.axis_index("ctx")
@@ -79,15 +80,25 @@
     for to in [at((z + d) % planes, p) for d, p in line] + [x_mate, y_mate]:
         pl.semaphore_signal(barrier, inc=1, device_id=to, device_id_type=MESH)
 
-    parts = ((gate_hbm, gate_ref), (up_hbm, up_ref), (down_hbm, down_ref))
+    sources = (gate_hbm, up_hbm, down_hbm)
+
+    def weight_ref(i, e, place):
+        if i == 2:
+            return down_ref.at[e, place]
+        return both_ref.at[e, place, i * wide : (i + 1) * wide]
+
+    inputs = (
+        (cot_hbm, cot_ref),
+        (tok_hbm, rows_in.at[0, z, 0:rows]),
+    ) + tuple(
+        (sources[i].at[0], weight_ref(i, 0, pl.ds(0, sources[i].shape[1]))) for i in range(3)
+    )
     loads = [
-        pltpu.make_async_copy(src.at[0], dst.at[0], load_sems.at[i])
-        for i, (src, dst) in enumerate(parts)
+        pltpu.make_async_copy(src, dst, load_sems.at[i]) for i, (src, dst) in enumerate(inputs)
     ]
     for load in loads:
         load.start()
 
-    rows_in[0, z, 0:rows, :] = tok_ref[...]
     place = me * rows + lax.broadcasted_iota(jnp.int32, (rows, 128), 0)
     own_length = jnp.zeros((rows, 128), jnp.int32)
     begin = jnp.int32(0)
@@ -96,8 +107,10 @@
         own_length = jnp.where((place >= begin) & (place < begin + size), size, own_length)
         begin = begin + size
     loss_weight = (mean_length / own_length.astype(F32))[:, 0:1]
+    loads[0].wait()
     rows_in[1, z, 0:rows, :] = (cot_ref[...].astype(F32) * loss_weight).astype(BF16)
 
+    loads[1].wait()
     pl.semaphore_wait(barrier, len(line) + 2)
 
     def ag_copy(a, slot, to):
@@ -141,13 +154,13 @@
         )
 
     def half_of(i, which):
-        count = parts[i][1].shape[1] // 2
+        count = sources[i].shape[1] // 2
         return pl.ds(pl.multiple_of(which * count, count), count)
 
     def x_copy(i):
         return pltpu.make_async_remote_copy(
-            src_ref=parts[i][0].at[0, half_of(i, group)],
-            dst_ref=parts[i][1].at[1, half_of(i, group)],
+            src_ref=sources[i].at[0, half_of(i, group)],
+            dst_ref=weight_ref(i, 1, half_of(i, group)),
             send_sem=x_send.at[i],
             recv_sem=x_recv.at[i],
             device_id=x_mate,
@@ -156,8 +169,8 @@
 
     def y_copy(i):
         return pltpu.make_async_remote_copy(
-            src_ref=parts[i][1].at[1, half_of(i, group)],
-            dst_ref=parts[i][1].at[1, half_of(i, group)],
+            src_ref=weight_ref(i, 1, half_of(i, group)),
+            dst_ref=weight_ref(i, 1, half_of(i, group)),
             send_sem=y_send.at[i],
             recv_sem=y_recv.at[i],
             device_id=y_mate,
@@ -215,7 +228,7 @@
         w_copy(d, p).start()
     w_in[2 * z] = w_send[2 * z + core]
 
-    for load in loads:
+    for load in loads[2:]:
         load.wait()
     for a in range(2):
         pair_copy(a, z).wait_recv()
@@ -233,8 +246,8 @@
         x = rows_in[0, slot]
         g = rows_in[1, slot]
         weight = jnp.concatenate([column(slot, 0, whose), column(slot, 1, whose)], axis=0)
-        gate_pre = jnp.dot(x, gate_ref[e], preferred_element_type=F32)
-        up_value = jnp.dot(x, up_ref[e], preferred_element_type=F32)
+        both = jnp.dot(x, both_ref[e], preferred_element_type=F32)
+        gate_pre, up_value = both[:, 0:wide], both[:, wide : 2 * wide]
         hidden_grad = lax.dot_general(g, down_ref[e], NT, preferred_element_type=F32)
         sig = 0.5 * jnp.tanh(0.5 * gate_pre) + 0.5
         act = gate_pre * sig
@@ -248,8 +261,8 @@
         scaled = hidden_grad * weight
         gate_grad = (scaled * up_value * (sig * (1.0 + gate_pre * (1.0 - sig)))).astype(BF16)
         up_grad = (scaled * act).astype(BF16)
-        slot_grad = lax.dot_general(gate_grad, gate_ref[e], NT, preferred_element_type=F32)
-        slot_grad = slot_grad + lax.dot_general(up_grad, up_ref[e], NT, preferred_element_type=F32)
+        grads = jnp.concatenate([gate_grad, up_grad], axis=1)
+        slot_grad = lax.dot_general(grads, both_ref[e], NT, preferred_element_type=F32)
         if e == 0:
             acc[0, slot] = mix
             acc[1, slot] = slot_grad
@@ -347,30 +360,31 @@
     pass_on(2)
     for i in range(3):
         y_copy(i).wait_recv()
-    compute(1, turn(0))
-    arrivals(last)
     inner = (z > 0) & (z < last)
     high = z >= planes // 2
+
+    def second_pass(begin, end, wanted):
+        @pl.when(wanted)
+        def _():
+            @pl.loop(begin, end)
+            def _(j):
+                slot = 0
+                for jj in range(begin, end):
+                    slot = slot + turn(jj) * (j == jj).astype(jnp.int32)
+                compute(1, slot)
+
+    compute(1, turn(0))
+    second_pass(1, 4, inner)
     for k, u in enumerate(upward):
         line_step(planes - 1 - u, False, high)
         line_step(u, True, z >= 0)
         line_step(planes - 1 - u, False, z < planes // 2)
         if k == 0:
+            arrivals(last)
             first_pass(last)
-
-            @pl.loop(1, 4)
-            def _(j):
-                slot = 0
-                for jj in range(1, 4):
-                    slot = slot + turn(jj) * (j == jj).astype(jnp.int32)
-
-                @pl.when((j < 3) | inner)
-                def _():
-                    compute(1, slot)
+            second_pass(1, 3, (z == 0) | (z == last))
         elif k == 1:
-            @pl.when((z == 0) | (z == last))
-            def _():
-                compute(1, turn(3))
+            second_pass(3, 4, (z == 0) | (z == last))
         elif k + 2 < planes:
             compute(1, turn(k + 2))
     for d, p in line:
@@ -444,12 +458,12 @@
             jax.ShapeDtypeStruct(tokens.shape, BF16),
             jax.ShapeDtypeStruct((top, rows), F32),
         ),
-        in_specs=[pl.BlockSpec(memory_space=pltpu.SMEM)] + [vmem] * 4 + [hbm] * 3,
+        in_specs=[pl.BlockSpec(memory_space=pltpu.SMEM)] + [hbm] * 2 + [vmem] * 2 + [hbm] * 3,
         out_specs=(vmem, vmem, vmem),
         scratch_shapes=[
-            pltpu.VMEM((2, depth, hidden), BF16),
-            pltpu.VMEM((2, depth, hidden), BF16),
+            pltpu.VMEM((2, depth, 2 * hidden), BF16),
             pltpu.VMEM((2, hidden, depth), BF16),
+            pltpu.VMEM((rows, depth), BF16),
             pltpu.VMEM((2, planes, 2 * rows, depth), BF16),
             pltpu.VMEM((2, planes, 2 * rows, depth), F32),
             pltpu.VMEM((2, planes, 2 * rows, depth), BF16),
@@ -460,7 +474,7 @@
             pltpu.VMEM((rows, 8 * n), F32),
             pltpu.VMEM((n // 2, 2, 8, rows), F32),
             pltpu.VMEM((n // 2, 2, 8, rows), F32),
-            dma((3,)),
+            dma((5,)),
             dma((3,)),
             dma((3,)),
             dma((3,)),
@@ -477,7 +491,7 @@
             dma((2,)),
         ],
         compiler_params=pltpu.CompilerParams(
-            collective_id=0, has_side_effects=True, vmem_limit_bytes=52 * 1024 * 1024
+            collective_id=0, has_side_effects=True, vmem_limit_bytes=63 * 1024 * 1024
         ),
         cost_estimate=pl.CostEstimate(
             flops=12 * n * rows * w_gate.size, bytes_accessed=6 * w_gate.size, transcendentals=0

time: 107 us -> 103 us (0.963)
  local copies, waits for them, and re-layouts: 7.05 us -> 3.01 us
    unnamed x15 -> x7, local copies, waits for them, and re-layouts: 7.05 us -> 3.01 us
where the time goes in v3:
time: 103 us
  Pallas kernels  99.1 us (96%)
  local copies, waits for them, and re-layouts  3.01 us (3%)
    pallas_call x1, Pallas kernels, line_device(): pl.pallas_call(functools.partial(line_kernel, n, rows * 4.0), out_shape=(...  99.1 us
    unnamed x7, local copies, waits for them, and re-layouts  3.01 us

profile of v3, /device:TPU:0, one launch (start us, length us, event | category | flops | bytes accessed | tf_op | source)
XLA Modules:
  0.0 102.8 jit_solution(3849484717269145169)
XLA Ops:
  0.6 99.1 %shard_map.103 = (bf16[128,1024]{1,0:T(8,128)(2,1)}, bf16[128,1024]{1,0:T(8,128)(2,1)}, f32[8,128]{1,0:T(8,128)}) custom-call(s32[4]{0:T(128)} %seq_ref.1, bf16[128,1024]{1,0:T(8,128)(2,1)} %tok_hbm.1, bf16[128,1024]{1,0:T(8,128)(2,1)} %cot_hbm.1, s32[8,128]{1,0:T(8,128)} %bitcast.4, f32[8,128]{1,0:T(8,128)} %bitcast.5, bf16[1,1024,384]{2,1,0:T(8,128)(2,1)} %gate_hbm.1, ...), custom_call_target="tpu_custom_call" | custom-call | flops 9663676416 | bytes 2359296 | tf_op jit(solution)/shard_map/pallas_call | solution.py:454
  99.7 0.0 copy-start
  99.8 1.7 %copy.14 = bf16[128,1024]{1,0:T(8,128)(2,1)} copy(bf16[128,1024]{1,0:T(8,128)(2,1)} %get-tuple-element.12) | data formatting | bytes 524288
  101.5 0.0 copy-done
  101.5 0.0 copy-start.1
  101.5 0.7 copy.15
  102.2 0.0 copy-done.1
  102.2 0.6 copy.16
Async XLA Ops:
  99.7 1.7 %copy-start = (bf16[128,1024]{1,0:T(8,128)(2,1)S(1)}, bf16[128,1024]{1,0:T(8,128)(2,1)}, u32[]{:S(2)}) copy-start(bf16[128,1024]{1,0:T(8,128)(2,1)} %get-tuple-element.13) | copy-start | bytes 786436
  101.5 0.7 copy-start.1
